TPU v7x, 256 devices: a whole 4x4x8 slice. The times are simulated.
256 devices in a mesh: dp: 8 (over z), graph: 32 (over x, y, core).
Axes of the slice: x: 4, y: 4, z: 8, core: 2. Of those that a mesh axis runs over, the one named last changes fastest.
Arguments:
- node_feats: bfloat16 [8, 224, 49, 256], P('dp', 'graph'), may hold values from -0.125 to 0.125
- node_grads: bfloat16 [8, 224, 49, 256], P('dp', 'graph'), may hold values from -1.75 to 1.75
- node_row: int32 [8, 224], P('dp'), may hold values from 0 to 223, as said below
- edge_src: int32 [8, 16384], P('dp', 'graph'), may hold values from 0 to 223, as said below
- edge_tgt: int32 [8, 16384], P('dp', 'graph'), may hold values from 0 to 223, as said below
- edge_rot: int32 [8, 16384], P('dp', 'graph'), may hold values from 0 to 2047
- edge_len: float32 [8, 16384], P('dp', 'graph'), may hold values from 0.5 to 11.5
- edge_count: int32 [8, 32], P('dp', 'graph'), may hold values from 64 to 512, as said below
- rotations: bfloat16 [2048, 7, 49], replicated, as said below
- w_zero: bfloat16 [1792, 1792], replicated, may hold values from -0.125 to 0.125
- w_radial: float32 [600, 256], replicated, may hold values from -3 to 3
Outputs:
- node_grad: float32 [8, 224, 49, 256], P('dp', 'graph')
- weight_grad: float32 [1792, 1792], P('graph')
Inputs may be any that keep to these rules, and one draw needn't show every extreme that they name: Each row of node_row is a permutation: atom i of a batch graph is held at row node_row[b, i], and graph index g holds rows g * 7 to (g + 1) * 7 - 1. `edge_tgt`: for every slot of the block of graph index g, the target atom is held at one of the rows g * 7 to (g + 1) * 7 - 1. `edge_src`: among the 512 slots of the block of one index of graph, at most 24 have source atoms held by the same index of graph; in every batch graph one index of graph holds the source atoms of exactly 24 live slots of every block. The first edge_count[b, g] slots of a block are live, the others are padding with valid ids; in every batch graph one index of graph has all 512 slots live. `rotations`: row l of each rotation is zero outside the coefficients of degree l (coefficients l * l to l * l + 2 l).
All inputs are finite; a program needn't handle non-finite values.
Results may differ from a plain program's by a relative error of at most 0.0041.
Values may be sent and summed in bfloat16 or wider, within the bound.
A program may use at most 256 MiB of HBM per device.

v0:
```python
import jax
import jax.numpy as jnp
from jax import lax
from jax.sharding import PartitionSpec as P

BLOCK = 256
CUTOFF = 12.0


def radial_profile(lengths, w_radial):
    gauss_count = w_radial.shape[0]
    spacing = CUTOFF / (gauss_count - 1)
    centers = jnp.arange(gauss_count).astype(jnp.float32) * spacing
    basis = jnp.exp(-0.5 / (2.0 * spacing) ** 2 * (lengths[:, None] - centers[None, :]) ** 2)
    return jnp.dot(
        basis, w_radial, precision=lax.Precision.HIGHEST, preferred_element_type=jnp.float32
    )


def find_rows(atom_ids, row_table):
    matches = atom_ids[:, None] == jnp.arange(row_table.shape[0], dtype=jnp.int32)[None, :]
    return jnp.sum(jnp.where(matches, row_table[None, :], 0), axis=1)


def forward_rows(turning, source, radial):
    rotated = jnp.einsum("bij,bjc->bic", turning, source, preferred_element_type=jnp.float32)
    return (rotated * radial[:, None, :]).astype(jnp.bfloat16)


def backward_terms(edge_in, target, turning, radial, w_zero):
    edge_grad = jnp.einsum(
        "bij,bjc->bic", turning, target, preferred_element_type=jnp.float32
    ).astype(jnp.bfloat16)
    edge_rows = edge_in.shape[0]
    flat_in = edge_in.reshape(edge_rows, -1)
    flat_grad = edge_grad.reshape(edge_rows, -1)
    weight_term = lax.dot_general(
        flat_in, flat_grad, (((0,), (0,)), ((), ())), preferred_element_type=jnp.float32
    )
    hidden = lax.dot_general(
        flat_grad, w_zero, (((1,), (1,)), ((), ())), preferred_element_type=jnp.float32
    )
    returned = (hidden.reshape(edge_in.shape) * radial[:, None, :]).astype(jnp.bfloat16)
    return (weight_term, returned)


def spread_back(turning, returned):
    return jnp.einsum("bij,bic->bjc", turning, returned, preferred_element_type=jnp.float32)


def per_device(
    node_feats,
    node_grads,
    node_row,
    edge_src,
    edge_tgt,
    edge_rot,
    edge_len,
    edge_count,
    rotations,
    w_zero,
    w_radial,
):
    node_dev = node_feats.shape[1]
    own_index = lax.axis_index("graph")
    row_table = node_row[0]
    grad_table = node_grads[0]
    source_ids = edge_src[0]
    target_rows = find_rows(edge_tgt[0], row_table) - own_index * node_dev
    turn_ids = edge_rot[0]
    lengths = edge_len[0]
    live_count = edge_count[0, 0]
    source_rows = find_rows(source_ids, row_table)
    square = w_zero.shape[0]
    blocks = (live_count + BLOCK - 1) // BLOCK
    sources_all = lax.all_gather(node_feats, "graph", axis=1, tiled=True)[0]

    def advance(step_index, carry):
        weight_acc, node_acc = carry
        first = step_index * BLOCK
        here_source = lax.dynamic_slice_in_dim(source_rows, first, BLOCK)
        here_target = lax.dynamic_slice_in_dim(target_rows, first, BLOCK)
        here_turn = lax.dynamic_slice_in_dim(turn_ids, first, BLOCK)
        here_length = lax.dynamic_slice_in_dim(lengths, first, BLOCK)
        alive_mask = (first + jnp.arange(BLOCK, dtype=jnp.int32) < live_count).astype(jnp.float32)
        radial = radial_profile(here_length, w_radial) * alive_mask[:, None]
        turning = rotations[here_turn]
        edge_in = forward_rows(turning, sources_all[here_source], radial)
        weight_term, returned = backward_terms(
            edge_in, grad_table[here_target], turning, radial, w_zero
        )
        return (
            weight_acc + weight_term,
            node_acc.at[here_source].add(spread_back(turning, returned)),
        )

    start_state = (
        jnp.zeros((square, square), jnp.float32),
        jnp.zeros(sources_all.shape, jnp.float32),
    )
    weight_acc, node_acc = lax.fori_loop(0, blocks, advance, start_state)
    node_part = lax.psum_scatter(node_acc[None], "graph", scatter_dimension=1, tiled=True)
    rows_part = lax.psum_scatter(weight_acc, "graph", scatter_dimension=0, tiled=True)
    weight_grad = lax.psum(rows_part, "dp")
    return (node_part, weight_grad)


def solution(mesh):
    placed = (
        P("dp", "graph", None, None),
        P("dp", "graph", None, None),
        P("dp", None),
        P("dp", "graph"),
        P("dp", "graph"),
        P("dp", "graph"),
        P("dp", "graph"),
        P("dp", "graph"),
        P(),
        P(),
        P(),
    )
    return jax.shard_map(
        per_device,
        mesh=mesh,
        in_specs=placed,
        out_specs=(P("dp", "graph", None, None), P("graph", None)),
        check_vma=False,
    )
```

profile of v0, /device:TPU:2, one launch (start us, length us, event | category | flops | bytes accessed | tf_op | source)
XLA Modules:
  0.0 616.0 jit_solution(6712216942642518904)
XLA Ops:
  7.2 0.0 all-gather.2.cloned.1.call-start
  7.2 0.7 all-gather.2.cloned.1.call-update
  7.9 0.0 reduce-scatter.2.cloned.1.call-start
  8.6 5.6 copy.34
  14.2 0.9 select_reduce_fusion
  15.1 52.0 %all-gather.2.cloned.1.call-done = bf16[1,224,49,256]{3,2,0,1:T(8,128)(2,1)} async-done(((bf16[1,7,49,256]{3,2,0,1:T(8,128)(2,1)}), bf16[1,224,49,256]{3,2,0,1:T(8,128)(2,1)}) %all-gather.2.cloned.1.call-update) | async-done | bytes 5619728 | tf_op jit(solution)/shard_map/all_gather | solution.py:76
  67.1 5.5 broadcast_in_dim.44
  72.6 0.0 copy-start
  72.6 0.0 copy-start.2
  72.6 0.0 copy-start.3
  72.6 0.0 copy-start.4
  72.6 5.4 broadcast_in_dim.45
  78.0 0.0 copy-done
  78.1 0.0 copy-done.2
  78.1 0.0 copy-done.3
  78.1 0.0 copy-done.4
  78.1 100.3 %while.12 = (s32[]{:T(128)}, f32[1792,1792]{1,0:T(8,128)}, f32[224,49,256]{2,1,0:T(8,128)}, s32[]{:T(128)}, s32[512]{0:T(512)S(1)}, /*index=5*/bf16[2048,7,49]{2...) while((s32[]{:T(128)}, f32[1792,1792]{1,0:T(8,128)}, ...), condition=%wide.region_4.5_spmd, body=%wide.region_2.4_spmd.sunk | while | flops 3904316672 | bytes 142397968 | solution.py:101
  78.3 0.1 compare_select_fusion.5
  78.4 3.0 gather_fusion
  81.4 0.1 compare_select_fusion.6
  81.5 6.8 %gather_fusion.1 = bf16[256,49,256]{2,1,0:T(8,128)(2,1)} fusion(bf16[224,49,256]{2,1,0:T(8,128)(2,1)} %get-tuple-element.287, s32[1024]{0:T(1024)S(1)} %pad_clamp_fusion.7), kind=kCustom, calls=%fused_computation.1.clone.1 | custom fusion | bytes 12846080 | tf_op jit(solution)/shard_map/while/body/gather | solution.py:88
  88.3 0.1 dynamic_slice.20
  88.4 0.6 compare_convert_fusion.2
  89.0 0.9 convolution_multiply_fusion.2
  89.9 4.4 multiply_convert_fusion.2
  94.4 0.8 copy.49
  95.2 4.0 gather_fusion.2
  99.2 4.4 convolution_convert_fusion.2
  103.6 1.6 copy.50
  105.1 0.0 copy-start.1
  105.1 11.9 %convolution_add_fusion.2 = f32[1792,1792]{1,0:T(8,128)} fusion(f32[1792,1792]{1,0:T(8,128)} %get-tuple-element.263, bf16[256,1792]{0,1:T(8,128)(2,1)S(1)} %bitcast.58, bf16[256,1792]{0,1:T(8,128)(2,1)} %bitcast.59), kind=kOutput, calls=%fused_computation.4.clone.1 | convolution fusion | flops 1647378432 | bytes 27525120 | tf_op jit(solution)/shard_map/while/body/dot_general | solution.py:37
  117.0 0.0 copy-done.1
  117.0 4.7 fusion.49
  121.7 7.3 %fusion.50 = f32[256,49,256]{2,1,0:T(8,128)} fusion(bf16[256,7,49]{2,1,0:T(8,128)(2,1)S(1)} %gather_fusion, f32[256,7,256]{2,0,1:T(8,128)S(1)} %fusion.49, f32[256,256]{1,0:T(8,128)S(1)} %convolution_multiply_fusion.2), kind=kOutput, calls=%fused_computation.10.clone.1 | convolution fusion | flops 45875200 | bytes 15117824 | tf_op jit(solution)/shard_map/while/body/bij,bic->bjc/dot_general | solution.py:48
  129.0 0.0 copy-start.5
  129.1 49.3 %scatter_fusion = f32[224,49,256]{2,1,0:T(8,128)} fusion(f32[224,49,256]{2,1,0:T(8,128)} %get-tuple-element.264, s32[256]{0:T(256)S(1)} %get-tuple-element.242, f32[256,49,256]{2,1,0:T(8,128)} %fusion.50), kind=kCustom, calls=%fused_computation.3.clone.1 | custom fusion | flops 3211264 | bytes 38536192 | tf_op jit(solution)/shard_map/while/body/scatter-add | solution.py:94
  178.3 0.0 copy-done.5
  178.3 0.0 reduce-scatter.2.cloned.1.call-update
  178.3 0.0 all-reduce.6.cloned.1.call-start
  178.4 14.6 %copy.36 = f32[1,224,49,256]{3,0,2,1:T(1,128)} copy(f32[1,224,49,256]{3,2,1,0:T(8,128)} %bitcast.56) | data formatting | bytes 22478848 | tf_op jit(solution)/shard_map/broadcast_in_dim | solution.py:102
  193.0 0.0 copy-start.6
  193.0 0.0 all-reduce.6.cloned.1.call-update
  193.0 0.0 all-reduce.4.cloned.1.call-start
  193.1 197.9 %reduce-scatter.2.cloned.1.call-done = f32[56,1792]{1,0:T(8,128)} async-done(((f32[1792,1792]{1,0:T(8,128)}), f32[56,1792]{1,0:T(8,128)}) %reduce-scatter.2.cloned.1.call-update) | async-done | bytes 401424 | tf_op jit(solution)/shard_map/reduce_scatter | solution.py:103
  390.9 0.0 all-reduce.4.cloned.1.call-update
  391.0 0.0 copy-done.6
  391.0 0.6 dynamic-slice
  392.2 140.3 %all-reduce.6.cloned.1.call-done = f32[1,224,49,256]{3,0,2,1:T(1,128)} async-done(((f32[1,224,49,256]{3,0,2,1:T(1,128)}), f32[1,224,49,256]{3,0,2,1:T(1,128)}) %all-reduce.6.cloned.1.call-update) | async-done | bytes 11239440
  532.5 2.0 constant_dynamic-slice_fusion
  534.4 73.3 %all-reduce.4.cloned.1.call-done = f32[56,1792]{1,0:T(8,128)} async-done(((f32[56,1792]{1,0:T(8,128)}), f32[56,1792]{1,0:T(8,128)}) %all-reduce.4.cloned.1.call-update) | async-done | bytes 401424 | tf_op jit(solution)/shard_map/psum | solution.py:104
  607.7 1.8 copy.64
  (5 shorter events, 0.0 us)
Async XLA Ops:
  7.2 59.9 %all-gather.2.cloned.1.call-start = ((), (), s32[]{:S(2)}) async-start(), calls=%async_computation.1 | async-start | bytes 6623232 | tf_op jit(solution)/shard_map/all_gather | solution.py:76
  7.9 383.0 %reduce-scatter.2.cloned.1.call-start = ((), (), s32[]{:S(2)}) async-start(), calls=%async_computation.2 | async-start | bytes 13246464 | tf_op jit(solution)/shard_map/reduce_scatter | solution.py:103
  72.6 5.4 copy-start
  72.6 5.4 copy-start.2
  72.6 5.4 copy-start.3
  72.6 5.4 copy-start.4
  105.1 11.9 %copy-start.1 = (bf16[256,7,256]{0,2,1:T(8,128)(2,1)S(1)}, bf16[256,7,256]{0,2,1:T(8,128)(2,1)}, u32[]{:S(2)}) copy-start(bf16[256,7,256]{0,2,1:T(8,128)(2,1)} %copy.50) | copy-start | bytes 2752516 | tf_op jit(solution)/shard_map/while
  129.0 49.3 %copy-start.5 = (f32[600,256]{1,0:T(8,128)S(1)}, f32[600,256]{1,0:T(8,128)}, u32[]{:S(2)}) copy-start(f32[600,256]{1,0:T(8,128)} %get-tuple-element.334) | copy-start | bytes 1843204 | tf_op jit(solution)/shard_map/while
  178.3 354.2 %all-reduce.6.cloned.1.call-start = ((), (), s32[]{:S(2)}) async-start(), calls=%async_computation.4 | async-start | bytes 22478848
  193.0 198.0 %copy-start.6 = (u32[256]{0:T(256)S(1)}, u32[256]{0:T(256)}, u32[]{:S(2)}) copy-start(u32[256]{0:T(256)} %constant.58) | copy-start | bytes 3076
  193.0 414.7 %all-reduce.4.cloned.1.call-start = ((), (), s32[]{:S(2)}) async-start(), calls=%async_computation.3 | async-start | bytes 802816 | tf_op jit(solution)/shard_map/psum | solution.py:104
Sparse Core Ops, SparseCore 0:
  10.6 56.4 all-gather.1
  178.5 212.4 reduce-scatter.1
  394.4 137.9 all-reduce.5
  534.7 72.9 all-reduce.3
where the time goes:
time: 618 us; the launch traced here: 616 us
  waiting for transfers between devices  464 us (75%)
  local copies, waits for them, and re-layouts  51.7 us (8%)
  other arithmetic  51 us (8%)
  matrix products  33.7 us (5%)
  between operations  15.1 us (2%)
    reduce_scatter x1, waiting for transfers between devices, per_device(): lax.psum_scatter(weight_acc, 'graph', scatter_dimension=0, tiled=True)  198 us
    unnamed x5, waiting for transfers between devices  141 us
    psum x1, waiting for transfers between devices, per_device(): weight_grad = lax.psum(rows_part, 'dp')  73.3 us
    all_gather x1, waiting for transfers between devices, per_device(): sources_all = lax.all_gather(node_feats, 'graph', axis=1, tiled=True)[0]  52 us
    scatter-add x1, other arithmetic, advance(): node_acc.at[here_source].add(spread_back(turning, returned))  49.3 us
    broadcast_in_dim x1, local copies, waits for them, and re-layouts, per_device(): node_acc[None]  14.6 us
  transfers between devices with their start and end apart: 4, of which 4 were waited for; matrix products, arithmetic and copies ran while one was open for 4% of the time, Pallas kernels for 0%

commit v1 on v0

--- a/solution.py
+++ b/solution.py
@@ -5,6 +5,28 @@
 
 BLOCK = 256
 CUTOFF = 12.0
+
+
+def laid_out(blocks, dim):
+    shape = list(blocks.shape[1:])
+    shape[dim] *= blocks.shape[0]
+    return jnp.moveaxis(blocks, 0, dim).reshape(shape)
+
+
+def doubled(value, axis):
+    length = lax.axis_size(axis)
+    pieces = value[None]
+    for level in range(length.bit_length() - 1):
+        bit = 1 << level
+        theirs = lax.ppermute(pieces, axis, [(i, i ^ bit) for i in range(length)])
+        both = jnp.stack([pieces, theirs])
+        upper = lax.axis_index(axis) >> level & 1
+        pieces = jnp.where(upper == 0, both, both[::-1]).reshape(-1, *value.shape)
+    return pieces
+
+
+def gather_by_bits(x, axis, dim):
+    return laid_out(doubled(x, axis), dim)
 
 
 def radial_profile(lengths, w_radial):
@@ -73,7 +95,7 @@
     source_rows = find_rows(source_ids, row_table)
     square = w_zero.shape[0]
     blocks = (live_count + BLOCK - 1) // BLOCK
-    sources_all = lax.all_gather(node_feats, "graph", axis=1, tiled=True)[0]
+    sources_all = gather_by_bits(node_feats, "graph", 1)[0]
 
     def advance(step_index, carry):
         weight_acc, node_acc = carry

time: 618 us -> 704 us (1.14)
  waiting for transfers between devices: 464 us -> 524 us
  other arithmetic: 51 us -> 60.7 us
  starting transfers between devices: 0.16 us -> 9.03 us
  local copies, waits for them, and re-layouts: 51.7 us -> 59.5 us
    ppermute x0 -> x5, waiting for transfers between devices: none -> 110 us  [doubled(): theirs = lax.ppermute(pieces, axis, [(i, i ^ bit) for i in range(length)])]
    all_gather x1 -> x0, waiting for transfers between devices: 52 us -> none  [per_device(): sources_all = lax.all_gather(node_feats, 'graph', axis=1, tiled=True)[0]]
    ppermute x0 -> x5, starting transfers between devices: none -> 8.9 us  [doubled(): theirs = lax.ppermute(pieces, axis, [(i, i ^ bit) for i in range(length)])]
    another operation x0 -> x7, other arithmetic: none -> 8.54 us  [doubled(): both = jnp.stack([pieces, theirs])]
    unnamed x5 -> x4, waiting for transfers between devices: 141 us -> 140 us
  transfers between devices with their start and end apart: 4 -> 8, of which waited for: 4 -> 8; matrix products, arithmetic and copies ran while one was open for 4% -> 3% of each run, Pallas kernels for 0% -> 0%
where the time goes in v1:
time: 704 us; the launch traced here: 702 us
  waiting for transfers between devices  524 us (74%)
  other arithmetic  60.7 us (9%)
  local copies, waits for them, and re-layouts  59.5 us (8%)
  matrix products  33.7 us (5%)
  between operations  15.2 us (2%)
  starting transfers between devices  9.03 us (1%)
    reduce_scatter x1, waiting for transfers between devices, per_device(): lax.psum_scatter(weight_acc, 'graph', scatter_dimension=0, tiled=True)  200 us
    unnamed x4, waiting for transfers between devices  140 us
    ppermute x5, waiting for transfers between devices, doubled(): theirs = lax.ppermute(pieces, axis, [(i, i ^ bit) for i in range(length)])  110 us
    psum x1, waiting for transfers between devices, per_device(): weight_grad = lax.psum(rows_part, 'dp')  73.4 us
    scatter-add x1, other arithmetic, advance(): node_acc.at[here_source].add(spread_back(turning, returned))  49.3 us
    broadcast_in_dim x1, local copies, waits for them, and re-layouts, per_device(): node_acc[None]  14.6 us
  transfers between devices with their start and end apart: 8, of which 8 were waited for; matrix products, arithmetic and copies ran while one was open for 3% of the time, Pallas kernels for 0%

profile of v1, /device:TPU:2, one launch (start us, length us, event | category | flops | bytes accessed | tf_op | source)
XLA Modules:
  0.0 702.0 jit_solution(4415677559518326305)
XLA Ops:
  7.2 0.0 reduce-scatter.2.cloned.1.call-start
  7.2 0.1 collective-permute-start
  7.3 1.6 collective-permute-done
  9.0 1.0 pad_maximum_fusion.4
  9.9 0.1 fusion.13
  10.0 1.7 collective-permute-start.1
  11.7 9.8 %collective-permute-done.1 = bf16[2,1,7,49,256]{4,3,2,0,1:T(8,128)(2,1)S(1)} collective-permute-done((bf16[2,1,7,49,256]{4,3,2,0,1:T(8,128)(2,1)S(1)}, bf16[2,1,7,49,256]{4,3,2,0,1:T(8,128)(2,1)S(1)}, u32[]{:S(2)}, u32[]{:S(2)}) %collective-permute-start.1) | collective-permute-done | bytes 351264 | tf_op jit(solution)/shard_map/ppermute | solution.py:21
  21.4 0.1 pad_maximum_fusion.3
  21.5 0.1 reverse_select_fusion.3
  21.7 0.3 copy.65
  22.0 3.3 collective-permute-start.2
  25.2 0.3 copy.64
  25.5 15.0 %collective-permute-done.2 = bf16[4,1,7,49,256]{4,0,3,2,1:T(4,128)(2,1)S(1)} collective-permute-done((bf16[4,1,7,49,256]{4,0,3,2,1:T(4,128)(2,1)S(1)}, bf16[4,1,7,49,256]{4,0,3,2,1:T(4,128)(2,1)S(1)}, u32[]{:S(2)}, u32[]{:S(2)}) %collective-permute-start.2) | collective-permute-done | bytes 702496 | tf_op jit(solution)/shard_map/ppermute | solution.py:21
  40.5 1.0 pad_maximum_fusion.2
  41.5 0.5 reverse_select_fusion.2
  42.1 0.5 copy.53
  42.5 1.4 reshape.41
  44.0 2.3 collective-permute-start.3
  46.2 0.3 stack_reshape.14
  46.6 29.3 %collective-permute-done.3 = bf16[8,1,7,49,256]{4,0,3,2,1:T(8,128)(2,1)} collective-permute-done((bf16[8,1,7,49,256]{4,0,3,2,1:T(8,128)(2,1)}, bf16[8,1,7,49,256]{4,0,3,2,1:T(8,128)(2,1)}, u32[]{:S(2)}, u32[]{:S(2)}) %collective-permute-start.3) | collective-permute-done | bytes 1404960 | tf_op jit(solution)/shard_map/ppermute | solution.py:21
  75.9 1.6 pad_maximum_fusion.1
  77.5 0.0 copy-start.4
  77.5 0.0 copy-start.5
  77.5 0.0 copy-start.6
  77.6 2.5 copy_bitcast_fusion.1
  80.1 1.6 collective-permute-start.4
  82.3 5.5 copy.58
  87.9 0.0 copy-done.4
  87.9 0.2 select_reduce_fusion
  88.1 54.3 %collective-permute-done.4 = bf16[16,1,7,49,256]{4,0,3,2,1:T(8,128)(2,1)} collective-permute-done((bf16[16,1,7,49,256]{4,0,3,2,1:T(8,128)(2,1)}, bf16[16,1,7,49,256]{4,0,3,2,1:T(8,128)(2,1)}, u32[]{:S(2)}, u32[]{:S(2)}) %collective-permute-start.4) | collective-permute-done | bytes 2809888 | tf_op jit(solution)/shard_map/ppermute | solution.py:21
  142.4 2.3 pad_maximum_fusion
  144.7 1.2 reverse_select_fusion
  145.9 5.1 copy.66
  151.0 5.5 broadcast_in_dim.47
  156.6 5.4 broadcast_in_dim.48
  162.0 100.3 %while.12 = (s32[]{:T(128)}, f32[1792,1792]{1,0:T(8,128)}, f32[224,49,256]{2,1,0:T(8,128)}, s32[]{:T(128)}, s32[512]{0:T(512)S(1)}, /*index=5*/bf16[2048,7,49]{2...) while((s32[]{:T(128)}, f32[1792,1792]{1,0:T(8,128)}, ...), condition=%wide.region_4.5_spmd, body=%wide.region_2.4_spmd.sunk | while | flops 3904316672 | bytes 142397968 | solution.py:123
  162.2 0.1 compare_select_fusion.5
  162.3 3.0 gather_fusion
  165.4 0.1 compare_select_fusion.6
  165.4 6.8 gather_fusion.1
  172.3 0.1 dynamic_slice.20
  172.3 0.6 compare_convert_fusion.2
  173.0 0.9 convolution_multiply_fusion.2
  173.9 4.4 multiply_convert_fusion.2
  178.4 0.8 copy.80
  179.2 4.0 gather_fusion.2
  183.1 4.4 convolution_convert_fusion.2
  187.5 1.5 copy.81
  189.1 11.9 %convolution_add_fusion.2 = f32[1792,1792]{1,0:T(8,128)} fusion(f32[1792,1792]{1,0:T(8,128)} %get-tuple-element.281, bf16[256,1792]{0,1:T(8,128)(2,1)S(1)} %bitcast.78, bf16[256,1792]{0,1:T(8,128)(2,1)} %bitcast.79), kind=kOutput, calls=%fused_computation.4.clone.1 | convolution fusion | flops 1647378432 | bytes 27525120 | tf_op jit(solution)/shard_map/while/body/dot_general | solution.py:59
  201.0 4.7 fusion.51
  205.7 7.3 %fusion.52 = f32[256,49,256]{2,1,0:T(8,128)} fusion(bf16[256,7,49]{2,1,0:T(8,128)(2,1)S(1)} %gather_fusion, f32[256,7,256]{2,0,1:T(8,128)S(1)} %fusion.51, f32[256,256]{1,0:T(8,128)S(1)} %convolution_multiply_fusion.2), kind=kOutput, calls=%fused_computation.10.clone.1 | convolution fusion | flops 45875200 | bytes 15117824 | tf_op jit(solution)/shard_map/while/body/bij,bic->bjc/dot_general | solution.py:70
  213.0 49.3 %scatter_fusion = f32[224,49,256]{2,1,0:T(8,128)} fusion(f32[224,49,256]{2,1,0:T(8,128)} %get-tuple-element.282, s32[256]{0:T(256)S(1)} %get-tuple-element.260, f32[256,49,256]{2,1,0:T(8,128)} %fusion.52), kind=kCustom, calls=%fused_computation.3.clone.1 | custom fusion | flops 3211264 | bytes 38536192 | tf_op jit(solution)/shard_map/while/body/scatter-add | solution.py:116
  262.3 0.0 reduce-scatter.2.cloned.1.call-update
  262.3 0.0 all-reduce.6.cloned.1.call-start
  262.3 14.6 %copy.61 = f32[1,224,49,256]{3,0,2,1:T(1,128)} copy(f32[1,224,49,256]{3,2,1,0:T(8,128)} %bitcast.76) | data formatting | bytes 22478848 | tf_op jit(solution)/shard_map/broadcast_in_dim | solution.py:124
  277.0 0.0 all-reduce.6.cloned.1.call-update
  277.0 0.0 all-reduce.4.cloned.1.call-start
  277.0 200.0 %reduce-scatter.2.cloned.1.call-done = f32[56,1792]{1,0:T(8,128)} async-done(((f32[1792,1792]{1,0:T(8,128)}), f32[56,1792]{1,0:T(8,128)}) %reduce-scatter.2.cloned.1.call-update) | async-done | bytes 401424 | tf_op jit(solution)/shard_map/reduce_scatter | solution.py:125
  477.0 0.0 all-reduce.4.cloned.1.call-update
  477.0 0.6 dynamic-slice
  478.3 140.1 %all-reduce.6.cloned.1.call-done = f32[1,224,49,256]{3,0,2,1:T(1,128)} async-done(((f32[1,224,49,256]{3,0,2,1:T(1,128)}), f32[1,224,49,256]{3,0,2,1:T(1,128)}) %all-reduce.6.cloned.1.call-update) | async-done | bytes 11239440
  618.3 2.0 constant_dynamic-slice_fusion
  620.3 73.4 %all-reduce.4.cloned.1.call-done = f32[56,1792]{1,0:T(8,128)} async-done(((f32[56,1792]{1,0:T(8,128)}), f32[56,1792]{1,0:T(8,128)}) %all-reduce.4.cloned.1.call-update) | async-done | bytes 401424 | tf_op jit(solution)/shard_map/psum | solution.py:126
  693.7 1.8 copy.95
  (21 shorter events, 0.1 us)
Async XLA Ops:
  7.2 469.8 %reduce-scatter.2.cloned.1.call-start = ((), (), s32[]{:S(2)}) async-start(), calls=%async_computation.1 | async-start | bytes 13246464 | tf_op jit(solution)/shard_map/reduce_scatter | solution.py:125
  7.2 1.7 collective-permute-start
  10.0 11.4 %collective-permute-start.1 = (bf16[2,1,7,49,256]{4,3,2,0,1:T(8,128)(2,1)S(1)}, bf16[2,1,7,49,256]{4,3,2,0,1:T(8,128)(2,1)S(1)}, u32[]{:S(2)}, u32[]{:S(2)}) collective-permute-start(bf16[2,1,7,49,256]{4,3,2,0,1:T(8,128)(2,1)S(1)} %get-tuple-element.171), channel_id=1, source_target_pairs={{0,2},{1,3},{2,0},{3,1},{4,6},{5,7},{6,4},{7,5},{8,10},{9,11},{10,... | collective-permute-start | bytes 1053704 | tf_op jit(solution)/shard_map/ppermute | solution.py:21
  22.0 18.5 %collective-permute-start.2 = (bf16[4,1,7,49,256]{4,0,3,2,1:T(4,128)(2,1)S(1)}, bf16[4,1,7,49,256]{4,0,3,2,1:T(4,128)(2,1)S(1)}, u32[]{:S(2)}, u32[]{:S(2)}) collective-permute-start(bf16[4,1,7,49,256]{4,0,3,2,1:T(4,128)(2,1)S(1)} %copy.65), channel_id=1, source_target_pairs={{0,4},{1,5},{2,6},{3,7},{4,0},{5,1},{6,2},{7,3},{8,12},{9,13},{10,... | collective-permute-start | bytes 2107400 | tf_op jit(solution)/shard_map/ppermute | solution.py:21
  44.0 31.9 %collective-permute-start.3 = (bf16[8,1,7,49,256]{4,0,3,2,1:T(8,128)(2,1)}, bf16[8,1,7,49,256]{4,0,3,2,1:T(8,128)(2,1)}, u32[]{:S(2)}, u32[]{:S(2)}) collective-permute-start(bf16[8,1,7,49,256]{4,0,3,2,1:T(8,128)(2,1)} %reshape.41), channel_id=1, source_target_pairs={{0,8},{1,9},{2,10},{3,11},{4,12},{5,13},{6,14},{7,15},{8,0},{9,1},... | collective-permute-start | bytes 4214792 | tf_op jit(solution)/shard_map/ppermute | solution.py:21
  77.5 10.3 %copy-start.4 = (s32[1,512]{1,0:T(1,128)S(1)}, s32[1,512]{1,0:T(1,128)}, u32[]{:S(2)}) copy-start(s32[1,512]{1,0:T(1,128)} %param.17) | copy-start | bytes 6148
  77.5 10.3 %copy-start.5 = (s32[1,512]{1,0:T(1,128)S(1)}, s32[1,512]{1,0:T(1,128)}, u32[]{:S(2)}) copy-start(s32[1,512]{1,0:T(1,128)} %param.16) | copy-start | bytes 6148
  77.5 10.3 %copy-start.6 = (s32[1,224]{1,0:T(1,128)S(1)}, s32[1,224]{1,0:T(1,128)}, u32[]{:S(2)}) copy-start(s32[1,224]{1,0:T(1,128)} %param.15) | copy-start | bytes 2692
  80.1 62.4 %collective-permute-start.4 = (bf16[16,1,7,49,256]{4,0,3,2,1:T(8,128)(2,1)}, bf16[16,1,7,49,256]{4,0,3,2,1:T(8,128)(2,1)}, u32[]{:S(2)}, u32[]{:S(2)}) collective-permute-start(bf16[16,1,7,49,256]{4,0,3,2,1:T(8,128)(2,1)} %get-tuple-element.169), channel_id=1, source_target_pairs={{0,16},{1,17},{2,18},{3,19},{4,20},{5,21},{6,22},{7,23},{8,24},{9,... | collective-permute-start | bytes 8429576 | tf_op jit(solution)/shard_map/ppermute | solution.py:21
  156.6 5.4 copy-start
  156.6 5.4 copy-start.2
  156.6 5.4 copy-start.3
  156.6 5.4 copy-start.7
  189.1 11.9 %copy-start.1 = (bf16[256,7,256]{0,2,1:T(8,128)(2,1)S(1)}, bf16[256,7,256]{0,2,1:T(8,128)(2,1)}, u32[]{:S(2)}) copy-start(bf16[256,7,256]{0,2,1:T(8,128)(2,1)} %copy.81) | copy-start | bytes 2752516 | tf_op jit(solution)/shard_map/while
  213.0 49.3 %copy-start.8 = (f32[600,256]{1,0:T(8,128)S(1)}, f32[600,256]{1,0:T(8,128)}, u32[]{:S(2)}) copy-start(f32[600,256]{1,0:T(8,128)} %get-tuple-element.354) | copy-start | bytes 1843204 | tf_op jit(solution)/shard_map/while
  262.3 356.1 %all-reduce.6.cloned.1.call-start = ((), (), s32[]{:S(2)}) async-start(), calls=%async_computation.3 | async-start | bytes 22478848
  276.9 200.1 %copy-start.9 = (u32[256]{0:T(256)S(1)}, u32[256]{0:T(256)}, u32[]{:S(2)}) copy-start(u32[256]{0:T(256)} %constant.64) | copy-start | bytes 3076
  277.0 416.7 %all-reduce.4.cloned.1.call-start = ((), (), s32[]{:S(2)}) async-start(), calls=%async_computation.2 | async-start | bytes 802816 | tf_op jit(solution)/shard_map/psum | solution.py:126
Sparse Core Ops, SparseCore 0:
  262.4 214.5 reduce-scatter.1
  480.5 137.8 all-reduce.5
  620.7 72.9 all-reduce.3
